TPU v7x, 32 devices: a whole 2x2x4 slice. The times are simulated.
32 devices in a mesh: band: 4 (over x, core), inp: 8 (over z, y).
Axes of the slice: x: 2, y: 2, z: 4, core: 2. Of those that a mesh axis runs over, the one named last changes fastest.
Arguments:
- spectra: float32 [1024, 512, 256], P('inp', 'band'), parts along dimension 1, may hold values from -6 to 6
- delays: int32 [1024], replicated, may hold values from 0 to 127
- owner_bounds: int32 [9], replicated, may hold values from 0 to 4608, as said below
Outputs:
- owned: float32 [128, 7680, 256], P('band', 'inp'), parts along dimension 0
There are 4 independent parts, one for each index of `band`. A program takes and returns all parts, laid end to end along the dimension named above; an argument that names none is the same for every part. Nothing has to cross between parts.
Inputs may be any that keep to these rules, and one draw needn't show every extreme that they name: owner_bounds[0] = 0, owner_bounds[8] = 4608, rising; each owner_bounds[k] lies within 192 of k * 576; every owner holds at most 960 rows and some owner exactly 960.
All inputs are finite; a program needn't handle non-finite values.
Results may differ from a plain program's by a relative error of at most 0.000086.
Values sent between devices are 32-bit elements; how exact they have to be, the bound alone decides.
A program may use at most 256 MiB of HBM per device.

v0:
```python
import math
import jax
import jax.numpy as jnp
from jax import lax
from jax.sharding import PartitionSpec as P

CH = 128
AVG = 4
TILE = 128


def cross_product(left_side, right_side):
    return lax.dot_general(
        left_side,
        right_side,
        (((1,), (1,)), ((), ())),
        precision=lax.Precision.HIGHEST,
        preferred_element_type=jnp.float32,
    )


def pack_tile_rows(real_rows, imag_rows, row_tile):
    pieces = []
    for col_tile in range(row_tile + 1):
        pieces.append(
            jnp.concatenate(
                [
                    real_rows[:, col_tile * TILE : (col_tile + 1) * TILE],
                    imag_rows[:, col_tile * TILE : (col_tile + 1) * TILE],
                ],
                axis=1,
            )
        )
    return jnp.concatenate(pieces, axis=0)


def correct(turned, delays, first_chan):
    inputs, local_chans, row_len = turned.shape
    samples = row_len // 2
    channel = first_chan + jnp.arange(local_chans, dtype=jnp.int32)
    phase_steps = delays[:, None] * channel[None, :] % CH
    phase_angle = (phase_steps.astype(jnp.float32) * (2.0 * math.pi / CH))[:, :, None]
    cos_part = jnp.cos(phase_angle)
    sine_part = jnp.sin(phase_angle)
    real_part = turned[:, :, :samples]
    imag_part = turned[:, :, samples:]
    fixed_re = real_part * cos_part + imag_part * sine_part
    fixed_im = imag_part * cos_part - real_part * sine_part
    local_vis = local_chans // AVG
    direct = jnp.concatenate([fixed_re, fixed_im], axis=2).reshape(inputs, local_vis, AVG * row_len)
    swapped = jnp.concatenate([fixed_im, -fixed_re], axis=2).reshape(
        inputs, local_vis, AVG * row_len
    )
    return (direct, swapped)


def per_device(spectra, delays, owner_bounds):
    n_devices = lax.axis_size("inp")
    my_index = lax.axis_index("inp")
    turned = lax.all_to_all(spectra, "inp", split_axis=1, concat_axis=0, tiled=True)
    inputs, local_chans, row_len = turned.shape
    samples = row_len // 2
    norm_scale = 1.0 / (AVG * samples)
    direct, swapped = correct(turned, delays, my_index * local_chans)
    local_vis = local_chans // AVG
    tile_count = inputs // TILE
    packed_list = []
    for vis_index in range(local_vis):
        left_all = direct[:, vis_index]
        swap_all = swapped[:, vis_index]
        pieces = []
        square_re = cross_product(left_all, left_all) * norm_scale
        square_im = cross_product(swap_all, left_all) * norm_scale
        for row_tile in range(tile_count):
            pieces.append(
                pack_tile_rows(
                    square_re[row_tile * TILE : (row_tile + 1) * TILE],
                    square_im[row_tile * TILE : (row_tile + 1) * TILE],
                    row_tile,
                )
            )
        packed_list.append(jnp.concatenate(pieces, axis=0))
    packed = jnp.stack(packed_list, axis=0)
    rows_total = packed.shape[1]
    block_rows = rows_total // n_devices
    margin_rows = block_rows // 3
    slot_rows = block_rows + 2 * margin_rows
    slot_ids = jnp.arange(slot_rows, dtype=jnp.int32)
    counts = owner_bounds[1:] - owner_bounds[:-1]
    is_live = slot_ids[None, :] < counts[:, None]
    row_index = jnp.where(is_live, owner_bounds[:-1, None] + slot_ids[None, :], 0).reshape(-1)
    picked = jnp.take(packed, row_index, axis=1)
    outgoing = jnp.where(is_live.reshape(-1)[None, :, None], picked, jnp.zeros_like(picked))
    result = lax.all_to_all(outgoing, "inp", split_axis=1, concat_axis=0, tiled=True)
    return result


def solution(mesh):
    placed = (P("inp", "band", None), P(), P())
    return jax.shard_map(
        per_device, mesh=mesh, in_specs=placed, out_specs=P("band", "inp", None), check_vma=False
    )
```

profile of v0, /device:TPU:0, one launch (start us, length us, event | category | flops | bytes accessed | tf_op | source)
XLA Modules:
  0.0 1490.5 jit_solution(15595072913385701790)
XLA Ops:
  0.0 17.8 %copy.17 = f32[128,128,256]{2,0,1:T(8,128)} copy(f32[128,128,256]{2,1,0:T(8,128)} %param.3) | data formatting | bytes 33554432 | tf_op args[0]
  17.8 7.8 all-to-all-start
  25.6 0.0 copy-done.54
  25.6 0.3 fusion.68
  25.9 0.2 copy.20
  26.1 0.2 copy.21
  26.4 0.1 slice_subtract_fusion
  26.4 0.1 iota_add_fusion
  26.5 0.1 select_n.61
  26.6 0.1 add.74
  26.7 0.1 iota_compare_fusion
  26.8 0.1 lt.59
  26.9 0.1 fusion.69
  27.0 0.6 pad_clamp_fusion
  27.6 0.6 compare_and_fusion
  28.2 360.2 %all-to-all-done = f32[128,128,256]{2,0,1:T(8,128)} async-done(((f32[128,128,256]{2,0,1:T(8,128)}), f32[128,128,256]{2,0,1:T(8,128)}, u32[]{:S(2)}, u32[]{:S(2)}) %all-to-all-start) | async-done | bytes 16777248 | tf_op jit(solution)/shard_map/all_to_all | solution.py:60
  388.4 15.2 %copy.19 = f32[8,128,16,256]{3,2,1,0:T(8,128)S(1)} copy(f32[8,128,16,256]{3,1,2,0:T(8,128)} %bitcast.2) | data formatting | bytes 33554432 | tf_op jit(solution)/shard_map/all_to_all | solution.py:60
  403.7 8.2 fusion.70
  411.9 17.4 %pad_maximum_fusion.2 = (f32[1024,16,256]{2,1,0:T(8,128)}, f32[1024,16,256]{2,1,0:T(8,128)}) fusion(f32[1024,16,128]{2,1,0:T(8,128)S(1)} %get-tuple-element.5, f32[1024,16,128]{2,1,0:T(8,128)} %get-tuple-element.7, f32[1024,16,128]{2,1,0:T(8,128)S(1)} %get-tuple-element.6), kind=kLoop, calls=%fused_computation.4 | loop fusion | flops 8388608 | bytes 58720256 | tf_op jit(solution)/shard_map/concatenate | solution.py:51
  429.3 20.4 %reshape.164 = f32[1024,4,1024]{2,1,0:T(4,128)} reshape(f32[1024,16,256]{2,1,0:T(8,128)} %get-tuple-element.17) | data formatting | bytes 33554432 | tf_op jit(solution)/shard_map/reshape | solution.py:50
  449.7 20.4 %reshape.165 = f32[1024,4,1024]{2,1,0:T(4,128)} reshape(f32[1024,16,256]{2,1,0:T(8,128)} %get-tuple-element.16) | data formatting | bytes 33554432 | tf_op jit(solution)/shard_map/reshape | solution.py:51
  470.0 70.8 %fusion.71 = (f32[1024,1,1024]{2,1,0:T(1,128)}, f32[1024,1,1024]{2,1,0:T(1,128)S(1)}, f32[1024,1,1024]{2,1,0:T(1,128)}, f32[1024,1,1024]{2,1,0:T(1,128)}, f32[10...) fusion(f32[1024,4,1024]{2,1,0:T(4,128)} %reshape.165, ...), kind=kLoop, calls=%fused_computation.212 | loop fusion | bytes 67108864 | tf_op jit(solution)/shard_map/slice | solution.py:70
  540.8 0.0 copy-start.4
  540.8 19.0 %fusion.32 = f32[1024,1024]{0,1:T(8,128)S(1)} fusion(f32[1024,1,1024]{2,1,0:T(1,128)} %get-tuple-element.315), kind=kOutput, calls=%fused_computation.39 | convolution fusion | flops 12885950464 | bytes 8388608 | tf_op jit(solution)/shard_map/dot_general | solution.py:13
  559.9 14.3 fusion.44
  574.2 0.0 copy-start.3
  574.2 1.0 fusion.76
  575.1 0.1 fusion.74
  575.3 1.1 fusion.75
  576.4 0.8 fusion.73
  577.2 14.3 fusion.35
  591.5 14.7 fusion.49
  606.2 0.7 fusion.80
  607.0 0.1 fusion.78
  607.1 0.8 fusion.79
  607.9 0.1 fusion.77
  608.0 0.5 copy-done.1
  608.7 14.3 fusion.38
  623.0 14.5 fusion.54
  637.5 0.8 fusion.84
  638.2 0.1 fusion.82
  638.4 0.7 fusion.83
  639.1 0.1 fusion.81
  639.3 14.7 fusion.41
  654.0 14.4 fusion.59
  668.4 0.0 copy-start.36
  668.4 0.0 copy-start.47
  668.4 0.0 copy-start.48
  668.4 0.0 copy-start.49
  668.5 0.0 copy-start.32
  668.5 0.0 copy-start.46
  668.5 0.1 fusion.88
  668.8 0.1 fusion.86
  669.0 0.1 fusion.87
  669.2 0.1 fusion.85
  669.4 0.9 constant_dynamic-update-slice_fusion.107
  670.5 0.2 constant_dynamic-update-slice_fusion.31
  673.7 6.9 pad_maximum_fusion
  680.7 21.5 %copy.22 = f32[4,4608,256]{2,0,1:T(4,128)} copy(f32[4,4608,256]{1,2,0:T(8,128)} %pad_maximum_fusion) | data formatting | bytes 37748736 | tf_op jit(solution)/shard_map/stack | solution.py:83
  702.2 36.3 %gather_fusion = f32[7680,4,256]{2,1,0:T(4,128)} fusion(f32[4,4608,256]{2,0,1:T(4,128)} %copy.22, s32[8192]{0:T(1024)S(1)} %copy-done.50), kind=kCustom, calls=%fused_computation | custom fusion | bytes 62945280 | tf_op jit(solution)/shard_map/jit(_take)/gather | solution.py:92
  738.5 40.9 %select_bitcast_fusion = f32[4,7680,256]{2,0,1:T(4,128)S(1)} fusion(f32[7680,4,256]{2,1,0:T(4,128)} %gather_fusion, pred[7680]{0:T(1024)(128)(4,1)S(1)} %copy-done.52, pred[7680]{0:T(1024)(128)(4,1)S(1)} %copy-done.53), kind=kLoop, calls=%fused_computation.1 | loop fusion | flops 15728640 | bytes 62929920 | tf_op jit(solution)/shard_map/jit(_where)/select_n | solution.py:93
  779.4 683.8 %all_to_all.36 = f32[4,7680,256]{2,0,1:T(4,128)} all-to-all(f32[4,7680,256]{2,0,1:T(4,128)S(1)} %select_bitcast_fusion), channel_id=1, replica_groups=mesh['band'=4,'inp'=8] {'inp'}, dimensions={1} | all-to-all | bytes 62914560 | tf_op jit(solution)/shard_map/all_to_all | solution.py:94
  1463.1 16.4 %copy.23 = f32[4,7680,256]{2,1,0:T(8,128)S(1)} copy(f32[4,7680,256]{2,0,1:T(4,128)} %all_to_all.36) | data formatting | bytes 62914560 | tf_op jit(solution)/shard_map/all_to_all | solution.py:94
  1479.6 10.7 copy.24
  (245 shorter events, 1.9 us)
Async XLA Ops:
  17.8 7.8 copy-start.54
  17.8 8.6 copy-start.55
  17.8 370.6 %all-to-all-start = ((f32[128,128,256]{2,0,1:T(8,128)}), f32[128,128,256]{2,0,1:T(8,128)}, u32[]{:S(2)}, u32[]{:S(2)}) async-start(f32[128,128,256]{2,0,1:T(8,128)} %copy.17), calls=%async_computation | async-start | bytes 33554432 | tf_op jit(solution)/shard_map/all_to_all | solution.py:60
  26.9 376.8 %copy-start.51 = (pred[7680]{0:T(1024)(128)(4,1)}, pred[7680]{0:T(1024)(128)(4,1)S(1)}, u32[]{:S(2)}) copy-start(pred[7680]{0:T(1024)(128)(4,1)S(1)} %lt.59) | copy-start | bytes 23044
  540.8 19.1 %copy-start.4 = (f32[1024,1,1024]{2,1,0:T(1,128)S(1)}, f32[1024,1,1024]{2,1,0:T(1,128)}, u32[]{:S(2)}) copy-start(f32[1024,1,1024]{2,1,0:T(1,128)} %get-tuple-element.8) | copy-start | bytes 12582916
  540.8 19.1 %copy-start.5 = (f32[1024,1,1024]{2,1,0:T(1,128)S(1)}, f32[1024,1,1024]{2,1,0:T(1,128)}, u32[]{:S(2)}) copy-start(f32[1024,1,1024]{2,1,0:T(1,128)} %get-tuple-element.315) | copy-start | bytes 12582916
  574.2 3.1 copy-start.3
  577.2 14.3 copy-start.2
  606.2 2.3 copy-start.1
  608.7 14.3 copy-start
  668.4 1.0 copy-start.36
  668.4 1.0 copy-start.47
  668.4 1.0 copy-start.48
  668.4 1.0 copy-start.49
  668.5 1.9 copy-start.32
  668.5 1.9 copy-start.46
  668.6 1.8 copy-start.30
  668.6 1.8 copy-start.45
  668.6 1.8 copy-start.28
  668.6 1.8 copy-start.44
  668.6 1.9 copy-start.26
  668.6 1.9 copy-start.43
  668.7 2.1 copy-start.24
  668.7 2.1 copy-start.42
  668.7 2.1 copy-start.22
  668.7 2.1 copy-start.41
  668.7 2.1 copy-start.20
  668.7 2.1 copy-start.40
  668.7 2.2 copy-start.18
  668.7 2.2 copy-start.39
  668.7 2.2 copy-start.15
  668.8 2.2 copy-start.38
  668.8 2.2 copy-start.12
  668.8 2.2 copy-start.37
  668.9 2.1 copy-start.9
  668.9 2.1 copy-start.35
  669.0 2.1 copy-start.6
  669.0 2.1 copy-start.34
  669.0 2.1 copy-start.33
  669.0 2.1 copy-start.31
  669.0 2.1 copy-start.29
  669.0 2.2 copy-start.27
  669.0 2.2 copy-start.25
  669.0 2.2 copy-start.23
  669.2 2.1 copy-start.21
  669.2 2.1 copy-start.19
  669.2 2.1 copy-start.17
  669.2 2.2 copy-start.14
  669.2 2.2 copy-start.11
  669.2 2.2 copy-start.8
  670.3 1.3 copy-start.16
  670.4 1.3 copy-start.13
  670.4 1.3 copy-start.10
  670.5 1.2 copy-start.7
  680.6 21.5 %copy-start.50 = (s32[8192]{0:T(1024)S(1)}, s32[8192]{0:T(1024)}, u32[]{:S(2)}) copy-start(s32[8192]{0:T(1024)} %pad_clamp_fusion) | copy-start | bytes 98308
  702.2 36.3 %copy-start.52 = (pred[7680]{0:T(1024)(128)(4,1)S(1)}, pred[7680]{0:T(1024)(128)(4,1)}, u32[]{:S(2)}) copy-start(pred[7680]{0:T(1024)(128)(4,1)} %copy-done.51) | copy-start | bytes 23044
  702.2 36.3 %copy-start.53 = (pred[7680]{0:T(1024)(128)(4,1)S(1)}, pred[7680]{0:T(1024)(128)(4,1)}, u32[]{:S(2)}) copy-start(pred[7680]{0:T(1024)(128)(4,1)} %compare_and_fusion) | copy-start | bytes 23044
where the time goes:
time: 1500 us; the launch traced here: 1490 us
  blocking collectives  684 us (46%)
  waiting for transfers between devices  360 us (24%)
  local copies, waits for them, and re-layouts  238 us (16%)
  matrix products  120 us (8%)
  other arithmetic  78.1 us (5%)
    all_to_all x1, blocking collectives, per_device(): lax.all_to_all(outgoing, 'inp', split_axis=1, concat_axis=0, tiled=True)  684 us
    all_to_all x1, waiting for transfers between devices, per_device(): lax.all_to_all(spectra, 'inp', split_axis=1, concat_axis=0, tiled=True)  360 us
    dot_general x8, matrix products, cross_product(): lax.dot_general(left_side, right_side, (((1,), (1,)), ((), ())), precisio...  120 us
    slice x1, local copies, waits for them, and re-layouts, per_device(): swap_all = swapped[:, vis_index]  70.8 us
    select_n x1, other arithmetic, per_device(): jnp.where(is_live.reshape(-1)[None, :, None], picked, jnp.zeros_like(pick...  40.9 us
    gather x1, local copies, waits for them, and re-layouts, per_device(): picked = jnp.take(packed, row_index, axis=1)  36.3 us
  transfers between devices with their start and end apart: 1, of which 1 were waited for; matrix products, arithmetic and copies ran while one was open for 0% of the time, Pallas kernels for 0%

commit v1 on v0

--- a/solution.py
+++ b/solution.py
@@ -57,7 +57,9 @@
 def per_device(spectra, delays, owner_bounds):
     n_devices = lax.axis_size("inp")
     my_index = lax.axis_index("inp")
-    turned = lax.all_to_all(spectra, "inp", split_axis=1, concat_axis=0, tiled=True)
+    parts = jnp.split(spectra, lax.axis_size("inp"), axis=1)
+    incoming = lax.all_to_all(jnp.stack(parts), "inp", 0, 0)
+    turned = jnp.concatenate(incoming, axis=0)
     inputs, local_chans, row_len = turned.shape
     samples = row_len // 2
     norm_scale = 1.0 / (AVG * samples)

time: 1500 us -> 1490 us (level)
    all_to_all x1 -> x0, local copies, waits for them, and re-layouts: 15.2 us -> none  [per_device(): lax.all_to_all(spectra, 'inp', split_axis=1, concat_axis=0, tiled=True)]
where the time goes in v1:
time: 1490 us; the launch traced here: 1480 us
  blocking collectives  684 us (46%)
  waiting for transfers between devices  360 us (24%)
  local copies, waits for them, and re-layouts  230 us (15%)
  matrix products  120 us (8%)
  other arithmetic  80.1 us (5%)
    all_to_all x1, blocking collectives, per_device(): lax.all_to_all(outgoing, 'inp', split_axis=1, concat_axis=0, tiled=True)  684 us
    all_to_all x1, waiting for transfers between devices, per_device(): incoming = lax.all_to_all(jnp.stack(parts), 'inp', 0, 0)  360 us
    dot_general x8, matrix products, cross_product(): lax.dot_general(left_side, right_side, (((1,), (1,)), ((), ())), precisio...  120 us
    slice x1, local copies, waits for them, and re-layouts, per_device(): swap_all = swapped[:, vis_index]  70.8 us
    select_n x1, other arithmetic, per_device(): jnp.where(is_live.reshape(-1)[None, :, None], picked, jnp.zeros_like(pick...  40.9 us
    gather x1, local copies, waits for them, and re-layouts, per_device(): picked = jnp.take(packed, row_index, axis=1)  36.3 us
  transfers between devices with their start and end apart: 1, of which 1 were waited for; matrix products, arithmetic and copies ran while one was open for 0% of the time, Pallas kernels for 0%

profile of v1, /device:TPU:0, one launch (start us, length us, event | category | flops | bytes accessed | tf_op | source)
XLA Modules:
  0.0 1483.9 jit_solution(11527213381192768272)
XLA Ops:
  0.0 3.1 bitcast_dynamic-update-slice_fusion.7
  3.1 3.1 bitcast_dynamic-update-slice_fusion.6
  6.2 3.1 bitcast_dynamic-update-slice_fusion.5
  9.3 3.1 bitcast_dynamic-update-slice_fusion.4
  12.4 3.1 bitcast_dynamic-update-slice_fusion.3
  15.5 3.1 bitcast_dynamic-update-slice_fusion.2
  18.6 3.1 bitcast_dynamic-update-slice_fusion.1
  21.7 3.1 bitcast_dynamic-update-slice_fusion
  24.8 7.4 all-to-all-start
  32.2 0.3 fusion.68
  32.5 0.2 copy.10
  32.8 0.2 copy.11
  33.0 0.1 slice_subtract_fusion
  33.0 0.1 iota_add_fusion
  33.1 0.1 select_n.61
  33.2 0.1 add.74
  33.3 0.1 iota_compare_fusion
  33.4 0.1 lt.59
  33.5 0.1 fusion.69
  33.6 0.6 pad_clamp_fusion
  34.2 0.6 compare_and_fusion
  34.8 360.3 %all-to-all-done = f32[8,128,16,256]{3,2,1,0:T(8,128)} async-done(((f32[8,128,16,256]{3,2,1,0:T(8,128)}), f32[8,128,16,256]{3,2,1,0:T(8,128)}, u32[]{:S(2)}, u32[]{:S(2)}) %all-to-all-start) | async-done | bytes 16777248 | tf_op jit(solution)/shard_map/all_to_all | solution.py:61
  395.1 10.3 fusion.70
  405.4 0.0 copy-done.51
  405.4 17.4 %pad_maximum_fusion.2 = (f32[1024,16,256]{2,1,0:T(8,128)}, f32[1024,16,256]{2,1,0:T(8,128)}) fusion(f32[1024,16,128]{2,1,0:T(8,128)S(1)} %get-tuple-element.5, f32[1024,16,128]{2,1,0:T(8,128)} %get-tuple-element.7, f32[1024,16,128]{2,1,0:T(8,128)S(1)} %get-tuple-element.6), kind=kLoop, calls=%fused_computation.4 | loop fusion | flops 8388608 | bytes 58720256 | tf_op jit(solution)/shard_map/concatenate | solution.py:51
  422.7 20.4 %reshape.168 = f32[1024,4,1024]{2,1,0:T(4,128)} reshape(f32[1024,16,256]{2,1,0:T(8,128)} %get-tuple-element.17) | data formatting | bytes 33554432 | tf_op jit(solution)/shard_map/reshape | solution.py:50
  443.1 20.4 %reshape.169 = f32[1024,4,1024]{2,1,0:T(4,128)} reshape(f32[1024,16,256]{2,1,0:T(8,128)} %get-tuple-element.16) | data formatting | bytes 33554432 | tf_op jit(solution)/shard_map/reshape | solution.py:51
  463.5 70.8 %fusion.71 = (f32[1024,1,1024]{2,1,0:T(1,128)}, f32[1024,1,1024]{2,1,0:T(1,128)S(1)}, f32[1024,1,1024]{2,1,0:T(1,128)}, f32[1024,1,1024]{2,1,0:T(1,128)}, f32[10...) fusion(f32[1024,4,1024]{2,1,0:T(4,128)} %reshape.169, ...), kind=kLoop, calls=%fused_computation.220 | loop fusion | bytes 67108864 | tf_op jit(solution)/shard_map/slice | solution.py:72
  534.3 0.0 copy-start.4
  534.3 19.0 %fusion.32 = f32[1024,1024]{0,1:T(8,128)S(1)} fusion(f32[1024,1,1024]{2,1,0:T(1,128)} %get-tuple-element.315), kind=kOutput, calls=%fused_computation.39 | convolution fusion | flops 12885950464 | bytes 8388608 | tf_op jit(solution)/shard_map/dot_general | solution.py:13
  553.3 0.0 copy-done.4
  553.3 14.3 fusion.44
  567.6 1.0 fusion.76
  568.5 0.1 fusion.74
  568.7 1.1 fusion.75
  569.8 0.8 fusion.73
  570.6 14.3 fusion.35
  584.9 14.7 fusion.49
  599.6 0.7 fusion.80
  600.4 0.1 fusion.78
  600.5 0.8 fusion.79
  601.3 0.1 fusion.77
  601.4 0.5 copy-done.1
  602.1 14.3 fusion.38
  616.4 14.5 fusion.54
  630.9 0.8 fusion.84
  631.6 0.1 fusion.82
  631.8 0.7 fusion.83
  632.5 0.1 fusion.81
  632.7 14.7 fusion.41
  647.4 14.4 fusion.59
  661.9 0.1 fusion.88
  662.2 0.1 fusion.86
  662.4 0.1 fusion.87
  662.6 0.1 fusion.85
  662.8 0.9 constant_dynamic-update-slice_fusion.107
  663.9 0.2 constant_dynamic-update-slice_fusion.31
  667.1 6.9 pad_maximum_fusion
  674.0 21.5 %copy.12 = f32[4,4608,256]{2,0,1:T(4,128)} copy(f32[4,4608,256]{1,2,0:T(8,128)} %pad_maximum_fusion) | data formatting | bytes 37748736 | tf_op jit(solution)/shard_map/stack | solution.py:85
  695.6 36.3 %gather_fusion = f32[7680,4,256]{2,1,0:T(4,128)} fusion(f32[4,4608,256]{2,0,1:T(4,128)} %copy.12, s32[8192]{0:T(1024)S(1)} %copy-done.50), kind=kCustom, calls=%fused_computation | custom fusion | bytes 62945280 | tf_op jit(solution)/shard_map/jit(_take)/gather | solution.py:94
  731.9 40.9 %select_bitcast_fusion = f32[4,7680,256]{2,0,1:T(4,128)S(1)} fusion(f32[7680,4,256]{2,1,0:T(4,128)} %gather_fusion, pred[7680]{0:T(1024)(128)(4,1)S(1)} %copy-done.52, pred[7680]{0:T(1024)(128)(4,1)S(1)} %copy-done.53), kind=kLoop, calls=%fused_computation.1 | loop fusion | flops 15728640 | bytes 62929920 | tf_op jit(solution)/shard_map/jit(_where)/select_n | solution.py:95
  772.8 683.7 %all_to_all.23 = f32[4,7680,256]{2,0,1:T(4,128)} all-to-all(f32[4,7680,256]{2,0,1:T(4,128)S(1)} %select_bitcast_fusion), channel_id=1, replica_groups=mesh['band'=4,'inp'=8] {'inp'}, dimensions={1} | all-to-all | bytes 62914560 | tf_op jit(solution)/shard_map/all_to_all | solution.py:96
  1456.5 16.4 %copy.13 = f32[4,7680,256]{2,1,0:T(8,128)S(1)} copy(f32[4,7680,256]{2,0,1:T(4,128)} %all_to_all.23) | data formatting | bytes 62914560 | tf_op jit(solution)/shard_map/all_to_all | solution.py:96
  1473.0 10.7 copy.14
  (251 shorter events, 1.9 us)
Async XLA Ops:
  24.8 7.4 copy-start.54
  24.8 8.2 copy-start.55
  24.8 370.3 %all-to-all-start = ((f32[8,128,16,256]{3,2,1,0:T(8,128)}), f32[8,128,16,256]{3,2,1,0:T(8,128)}, u32[]{:S(2)}, u32[]{:S(2)}) async-start(f32[8,128,16,256]{3,2,1,0:T(8,128)} %bitcast_dynamic-update-slice_fusion), calls=%async_computation | async-start | bytes 33554432 | tf_op jit(solution)/shard_map/all_to_all | solution.py:61
  33.5 371.9 %copy-start.51 = (pred[7680]{0:T(1024)(128)(4,1)}, pred[7680]{0:T(1024)(128)(4,1)S(1)}, u32[]{:S(2)}) copy-start(pred[7680]{0:T(1024)(128)(4,1)S(1)} %lt.59) | copy-start | bytes 23044
  534.3 19.0 %copy-start.4 = (f32[1024,1,1024]{2,1,0:T(1,128)S(1)}, f32[1024,1,1024]{2,1,0:T(1,128)}, u32[]{:S(2)}) copy-start(f32[1024,1,1024]{2,1,0:T(1,128)} %get-tuple-element.8) | copy-start | bytes 12582916
  534.3 19.0 %copy-start.5 = (f32[1024,1,1024]{2,1,0:T(1,128)S(1)}, f32[1024,1,1024]{2,1,0:T(1,128)}, u32[]{:S(2)}) copy-start(f32[1024,1,1024]{2,1,0:T(1,128)} %get-tuple-element.315) | copy-start | bytes 12582916
  567.6 3.1 copy-start.3
  570.6 14.3 copy-start.2
  599.6 2.3 copy-start.1
  602.1 14.3 copy-start
  661.8 1.0 copy-start.36
  661.8 1.0 copy-start.47
  661.8 1.0 copy-start.48
  661.8 1.0 copy-start.49
  661.9 1.9 copy-start.32
  661.9 1.9 copy-start.46
  662.0 1.8 copy-start.30
  662.0 1.8 copy-start.45
  662.0 1.8 copy-start.28
  662.0 1.8 copy-start.44
  662.0 1.9 copy-start.26
  662.0 1.9 copy-start.43
  662.1 2.1 copy-start.24
  662.1 2.1 copy-start.42
  662.1 2.1 copy-start.22
  662.1 2.1 copy-start.41
  662.1 2.1 copy-start.20
  662.1 2.1 copy-start.40
  662.1 2.2 copy-start.18
  662.1 2.2 copy-start.39
  662.1 2.2 copy-start.15
  662.1 2.2 copy-start.38
  662.2 2.2 copy-start.12
  662.2 2.2 copy-start.37
  662.3 2.1 copy-start.9
  662.3 2.1 copy-start.35
  662.3 2.1 copy-start.6
  662.4 2.1 copy-start.34
  662.4 2.1 copy-start.33
  662.4 2.1 copy-start.31
  662.4 2.1 copy-start.29
  662.4 2.2 copy-start.27
  662.4 2.2 copy-start.25
  662.4 2.2 copy-start.23
  662.6 2.1 copy-start.21
  662.6 2.1 copy-start.19
  662.6 2.1 copy-start.17
  662.6 2.2 copy-start.14
  662.6 2.2 copy-start.11
  662.6 2.2 copy-start.8
  663.7 1.3 copy-start.16
  663.8 1.3 copy-start.13
  663.8 1.3 copy-start.10
  663.9 1.2 copy-start.7
  674.0 21.5 %copy-start.50 = (s32[8192]{0:T(1024)S(1)}, s32[8192]{0:T(1024)}, u32[]{:S(2)}) copy-start(s32[8192]{0:T(1024)} %pad_clamp_fusion) | copy-start | bytes 98308
  695.6 36.3 %copy-start.52 = (pred[7680]{0:T(1024)(128)(4,1)S(1)}, pred[7680]{0:T(1024)(128)(4,1)}, u32[]{:S(2)}) copy-start(pred[7680]{0:T(1024)(128)(4,1)} %copy-done.51) | copy-start | bytes 23044
  695.6 36.3 %copy-start.53 = (pred[7680]{0:T(1024)(128)(4,1)S(1)}, pred[7680]{0:T(1024)(128)(4,1)}, u32[]{:S(2)}) copy-start(pred[7680]{0:T(1024)(128)(4,1)} %compare_and_fusion) | copy-start | bytes 23044
